TPU v7x, 512 devices: a whole 4x8x8 slice. The times are simulated.
512 devices in a mesh: dp: 2 (over core), expert: 32 (over z, x), tensor: 8 (over y).
Axes of the slice: x: 4, y: 8, z: 8, core: 2. Of those that a mesh axis runs over, the one named last changes fastest.
Arguments:
- grad_out: bfloat16 [8192, 4096], P(('dp', 'expert'), 'tensor'), may hold values from -6 to 6
- routes: int32 [8192, 8], P(('dp', 'expert')), may hold values from 0 to 31, as said below
- probs: bfloat16 [8192, 8], P(('dp', 'expert')), may hold values from 0.019897461 to 0.25
- vision: int32 [8192], P(('dp', 'expert')), may hold values from 0 to 1, as said below
- pre_text: bfloat16 [2, 32, 2, 32, 28, 1792], P('dp', 'expert', None, None, None, 'tensor'), may hold values from -6 to 6
- pre_vision: bfloat16 [2, 32, 2, 32, 28, 768], P('dp', 'expert', None, None, None, 'tensor'), may hold values from -6 to 6
- down_text: bfloat16 [32, 1792, 4096], P('expert', 'tensor', 'dp'), may hold values from -0.125 to 0.125
- down_vision: bfloat16 [32, 768, 4096], P('expert', 'tensor', 'dp'), may hold values from -0.21875 to 0.21875
Outputs:
- grad_pre_text: bfloat16 [2, 32, 2, 32, 28, 1792], P('dp', 'expert', None, None, None, 'tensor')
- grad_pre_vision: bfloat16 [2, 32, 2, 32, 28, 768], P('dp', 'expert', None, None, None, 'tensor')
- grad_down_text: bfloat16 [32, 1792, 4096], P('expert', 'tensor', 'dp')
- grad_down_vision: bfloat16 [32, 768, 4096], P('expert', 'tensor', 'dp')
- grad_probs: float32 [8192, 8], P(('dp', 'expert'))
Inputs may be any that keep to these rules, and one draw needn't show every extreme that they name: `routes`: each row names 8 different ids. Within one block of 128 tokens no id is named by more than 28 tokens of one modality; in each replica one text id and one vision id are named by exactly 28 tokens of that modality in every block of the replica. `vision`: in each block of 128 tokens the image patches form one run, cyclic within the block, of 28 to 100 positions.
All inputs are finite; a program needn't handle non-finite values.
Results may differ from a plain program's by a relative error of at most 0.0059.
Values may be sent and summed in bfloat16 or wider, within the bound.
A program may use at most 128 MiB of HBM per device.

v0:
```python
import jax
import jax.numpy as jnp
from jax import lax
from jax.sharding import PartitionSpec as P


def pair_positions(routes, vision, expert_total):
    expert_keys = (routes + expert_total * vision[:, None]).reshape(-1)
    onehot = (
        expert_keys[:, None] == jnp.arange(2 * expert_total, dtype=jnp.int32)[None, :]
    ).astype(jnp.int32)
    before = jnp.cumsum(onehot, axis=0) - onehot
    return jnp.sum(before * onehot, axis=1)


def saved_hidden(pre):
    saved = pre[0].astype(jnp.float32)
    gate_pre = saved[:, 0]
    up_pre = saved[:, 1]
    sigmoid_gate = jax.nn.sigmoid(gate_pre)
    return (gate_pre, up_pre, sigmoid_gate, gate_pre * sigmoid_gate * up_pre)


def family_grads(pre_parts, slot_weight, back_grad):
    gate_pre, up_pre, sigmoid_gate, hidden = pre_parts
    scaled = slot_weight[..., None] * back_grad
    grad_gate = scaled * up_pre * sigmoid_gate * (1.0 + gate_pre * (1.0 - sigmoid_gate))
    grad_up = scaled * gate_pre * sigmoid_gate
    grad_pre = jnp.stack([grad_gate, grad_up], axis=1).astype(jnp.bfloat16)[None]
    return (grad_pre, jnp.sum(hidden * back_grad, axis=-1))


def family_piece(back_grad, slot_rows, down_full, weighted):
    owners_here, rows_here, span_cols = slot_rows.shape
    per_owner = down_full.shape[0]
    shaped = slot_rows.reshape(owners_here, per_owner, rows_here // per_owner, span_cols)
    back_grad = jnp.einsum("secw,efw->escf", shaped, down_full, preferred_element_type=jnp.float32)
    update = jnp.einsum("escf,secw->efw", weighted, shaped, preferred_element_type=jnp.float32)
    return (back_grad, update)


def on_device(grad_out, routes, probs, vision, pre_text, pre_vision, down_text, down_vision):
    owners = lax.axis_size("expert")
    per_owner = down_text.shape[0]
    expert_total = per_owner * owners
    slot_cap = pre_text.shape[4]
    top_count = routes.shape[1]
    slot_total = expert_total * slot_cap
    position = pair_positions(routes, vision, expert_total)
    modality = jnp.repeat(vision, top_count)
    target = routes.reshape(-1) * slot_cap + position
    text_slot = jnp.where(modality == 0, target, slot_total)
    vision_slot = jnp.where(modality == 1, target, slot_total)
    pair_weight = probs.reshape(-1)
    whole_rows = lax.all_gather(grad_out, "tensor", axis=1, tiled=True)
    spread = jnp.repeat(whole_rows, top_count, axis=0)
    blank_rows = jnp.zeros((slot_total, whole_rows.shape[1]), whole_rows.dtype)
    blank_weight = jnp.zeros((slot_total,), pair_weight.dtype)
    text_rows = (
        blank_rows.at[text_slot].set(spread, mode="drop").reshape(owners, per_owner * slot_cap, -1)
    )
    vision_rows = (
        blank_rows.at[vision_slot]
        .set(spread, mode="drop")
        .reshape(owners, per_owner * slot_cap, -1)
    )
    text_weight = (
        blank_weight.at[text_slot]
        .set(pair_weight, mode="drop")
        .reshape(owners, per_owner * slot_cap)
    )
    vision_weight = (
        blank_weight.at[vision_slot]
        .set(pair_weight, mode="drop")
        .reshape(owners, per_owner * slot_cap)
    )
    text_rows, vision_rows, text_weight, vision_weight = (
        text_rows,
        vision_rows,
        text_weight,
        vision_weight,
    )
    received = (
        lax.all_to_all(text_rows, "expert", split_axis=0, concat_axis=0, tiled=True),
        lax.all_to_all(vision_rows, "expert", split_axis=0, concat_axis=0, tiled=True),
        lax.all_to_all(text_weight, "expert", split_axis=0, concat_axis=0, tiled=True),
        lax.all_to_all(vision_weight, "expert", split_axis=0, concat_axis=0, tiled=True),
    )
    full_text, full_vision = (
        lax.all_gather(down_text, "dp", axis=2, tiled=True),
        lax.all_gather(down_vision, "dp", axis=2, tiled=True),
    )
    text_parts = saved_hidden(pre_text)
    vision_parts = saved_hidden(pre_vision)

    def unpack_weight(received_weight):
        shaped = received_weight.reshape(owners, per_owner, slot_cap)
        return jnp.transpose(shaped, (1, 0, 2)).astype(jnp.float32)

    weight_text = unpack_weight(received[2])
    weight_vision = unpack_weight(received[3])
    weighted_text = (weight_text[..., None] * text_parts[3]).astype(jnp.bfloat16)
    weighted_vision = (weight_vision[..., None] * vision_parts[3]).astype(jnp.bfloat16)
    back_text = jnp.zeros(text_parts[3].shape, jnp.float32)
    back_vision = jnp.zeros(vision_parts[3].shape, jnp.float32)
    back_text, grad_text = family_piece(back_text, received[0], full_text, weighted_text)
    back_vision, grad_vision = family_piece(back_vision, received[1], full_vision, weighted_vision)
    back_text, back_vision, grad_text, grad_vision = (
        back_text,
        back_vision,
        grad_text,
        grad_vision,
    )
    grad_pre_text, score_text = family_grads(text_parts, weight_text, back_text)
    grad_pre_vision, score_vision = family_grads(vision_parts, weight_vision, back_vision)
    summed_text, summed_vision = (
        lax.psum_scatter(
            grad_text.astype(jnp.bfloat16), "dp", scatter_dimension=2, tiled=True
        ).astype(jnp.float32),
        lax.psum_scatter(
            grad_vision.astype(jnp.bfloat16), "dp", scatter_dimension=2, tiled=True
        ).astype(jnp.float32),
    )
    summed_scores = lax.psum((score_text, score_vision), "tensor")
    flat_text = jnp.transpose(summed_scores[0], (1, 0, 2)).reshape(owners, per_owner * slot_cap)
    flat_vision = jnp.transpose(summed_scores[1], (1, 0, 2)).reshape(owners, per_owner * slot_cap)
    chosen = jnp.where(
        modality == 0,
        lax.all_to_all(flat_text, "expert", split_axis=0, concat_axis=0, tiled=True).reshape(-1)[
            target
        ],
        lax.all_to_all(flat_vision, "expert", split_axis=0, concat_axis=0, tiled=True).reshape(-1)[
            target
        ],
    )
    grad_probs = chosen.reshape(routes.shape)
    return (
        grad_pre_text,
        grad_pre_vision,
        summed_text.astype(jnp.bfloat16),
        summed_vision.astype(jnp.bfloat16),
        grad_probs,
    )


def solution(mesh):
    in_specs = (
        P(("dp", "expert"), "tensor"),
        P(("dp", "expert"), None),
        P(("dp", "expert"), None),
        P(("dp", "expert")),
        P("dp", "expert", None, None, None, "tensor"),
        P("dp", "expert", None, None, None, "tensor"),
        P("expert", "tensor", "dp"),
        P("expert", "tensor", "dp"),
    )
    out_specs = (
        P("dp", "expert", None, None, None, "tensor"),
        P("dp", "expert", None, None, None, "tensor"),
        P("expert", "tensor", "dp"),
        P("expert", "tensor", "dp"),
        P(("dp", "expert"), None),
    )
    return jax.shard_map(
        on_device, mesh=mesh, in_specs=in_specs, out_specs=out_specs, check_vma=False
    )
```

profile of v0, /device:TPU:6, one launch (start us, length us, event | category | flops | bytes accessed | tf_op | source)
XLA Modules:
  0.0 595.3 jit_solution(2326108180317657653)
XLA Ops:
  11.4 0.8 copy.29
  12.6 18.0 %reduce-window.6 = s32[64,8,128]{2,1,0:T(8,128)S(1)} reduce-window(s32[64,8,128]{2,1,0:T(8,128)S(1)} %fusion.40, s32[]{:T(128)} %constant.9.clone.1), window={size=1x1x128 pad=0_0x0_0x127_0}, to_apply=%region_0.0 | reduce-window | flops 8323072 | bytes 524292 | tf_op jit(solution)/shard_map/reduce-window
  31.2 7.6 %scatter_custom_fusion = bf16[896]{0:T(1024)(128)(2,1)S(1)} fusion(s32[1024]{0:T(1024)S(1)} %bitcast.143, bf16[1024]{0:T(1024)(128)(2,1)S(1)} %reshape.435, bf16[]{:T(256)} %constant.8.clone.1), kind=kCustom, calls=%fused_computation.71 | custom fusion | bytes 1794 | tf_op jit(solution)/shard_map/scatter | solution.py:69
  38.8 0.7 all_to_all.40
  39.5 13.4 %all-to-all-start = ((bf16[32,1,28]{2,1,0:T(2,128)(2,1)}), bf16[32,1,28]{2,1,0:T(2,128)(2,1)S(1)}, u32[]{:S(2)}, u32[]{:S(2)}) async-start(bf16[32,1,28]{2,1,0:T(2,128)(2,1)} %all_to_all.40), calls=%async_computation | async-start | bytes 32768 | tf_op jit(solution)/shard_map/all_to_all | solution.py:86
  53.0 7.6 %scatter_custom_fusion.2 = bf16[896]{0:T(1024)(128)(2,1)S(1)} fusion(s32[1024]{0:T(1024)S(1)} %bitcast.145, bf16[1024]{0:T(1024)(128)(2,1)S(1)} %reshape.435, bf16[]{:T(256)} %constant.8.clone.1), kind=kCustom, calls=%fused_computation.69 | custom fusion | bytes 1794 | tf_op jit(solution)/shard_map/scatter | solution.py:74
  60.5 0.7 all_to_all.41
  61.3 10.1 %all-to-all-start.2 = ((bf16[32,1,28]{2,1,0:T(2,128)(2,1)}), bf16[32,1,28]{2,1,0:T(2,128)(2,1)S(1)}, u32[]{:S(2)}, u32[]{:S(2)}) async-start(bf16[32,1,28]{2,1,0:T(2,128)(2,1)} %all_to_all.41), calls=%async_computation.2 | async-start | bytes 32768 | tf_op jit(solution)/shard_map/all_to_all | solution.py:87
  71.4 16.0 %scatter_custom_fusion.3 = bf16[896,4096]{1,0:T(8,128)(2,1)} fusion(s32[1024]{0:T(1024)S(1)} %bitcast.146, bf16[128,4096]{1,0:T(8,128)(2,1)} %all-gather.3.cloned.1.call-done, bf16[]{:T(256)} %constant.8.clone.1), kind=kCustom, calls=%fused_computation.6 | custom fusion | bytes 8388610 | tf_op jit(solution)/shard_map/scatter | solution.py:64
  87.3 9.0 %reshape.389 = bf16[32,28,4096]{2,1,0:T(8,128)(2,1)} reshape(bf16[896,4096]{1,0:T(8,128)(2,1)} %scatter_custom_fusion.3) | data formatting | bytes 14680064 | tf_op jit(solution)/shard_map/reshape | solution.py:65
  96.3 10.4 %all-to-all-start.3 = ((bf16[32,28,4096]{2,1,0:T(8,128)(2,1)}), bf16[32,28,4096]{2,1,0:T(8,128)(2,1)}, u32[]{:S(2)}, u32[]{:S(2)}) async-start(bf16[32,28,4096]{2,1,0:T(8,128)(2,1)} %reshape.389), calls=%async_computation.3 | async-start | bytes 16777216 | tf_op jit(solution)/shard_map/all_to_all | solution.py:85
  106.7 15.5 %scatter_custom_fusion.1 = bf16[896,4096]{1,0:T(8,128)(2,1)} fusion(s32[1024]{0:T(1024)S(1)} %bitcast.144, bf16[128,4096]{1,0:T(8,128)(2,1)S(1)} %copy-done, bf16[]{:T(256)} %constant.8.clone.1), kind=kCustom, calls=%fused_computation.8 | custom fusion | bytes 8388610 | tf_op jit(solution)/shard_map/scatter | solution.py:60
  122.2 8.9 %reshape.387 = bf16[32,28,4096]{2,1,0:T(8,128)(2,1)} reshape(bf16[896,4096]{1,0:T(8,128)(2,1)} %scatter_custom_fusion.1) | data formatting | bytes 14680064 | tf_op jit(solution)/shard_map/reshape | solution.py:60
  131.2 162.6 %all-to-all-done.3 = bf16[32,28,4096]{2,1,0:T(8,128)(2,1)} async-done(((bf16[32,28,4096]{2,1,0:T(8,128)(2,1)}), bf16[32,28,4096]{2,1,0:T(8,128)(2,1)}, u32[]{:S(2)}, u32[]{:S(2)}) %all-to-all-start.3) | async-done | bytes 7340064 | tf_op jit(solution)/shard_map/all_to_all | solution.py:85
  293.7 8.1 %all-to-all-start.1 = ((bf16[32,28,4096]{2,1,0:T(8,128)(2,1)}), bf16[32,28,4096]{2,1,0:T(8,128)(2,1)}, u32[]{:S(2)}, u32[]{:S(2)}) async-start(bf16[32,28,4096]{2,1,0:T(8,128)(2,1)} %reshape.387), calls=%async_computation.1 | async-start | bytes 16777216 | tf_op jit(solution)/shard_map/all_to_all | solution.py:84
  303.1 8.7 %fusion.23 = bf16[1,96,4096]{2,1,0:T(8,128)(2,1)} fusion(bf16[32,28,4096]{2,1,0:T(8,128)(2,1)} %all-to-all-done.3, f32[32,28]{0,1:T(8,128)S(1)} %copy.34, f32[1,2,32,28,96]{4,2,3,1,0:T(8,128)S(1)} %bitcast_convert_fusion.1), kind=kOutput, calls=%fused_computation.19 | convolution fusion | flops 705638400 | bytes 8818176 | tf_op jit(solution)/shard_map/escf,secw->efw/dot_general | solution.py:38
  311.9 1.4 bitcast_convert_fusion
  313.5 177.0 %all-to-all-done.1 = bf16[32,28,4096]{2,1,0:T(8,128)(2,1)} async-done(((bf16[32,28,4096]{2,1,0:T(8,128)(2,1)}), bf16[32,28,4096]{2,1,0:T(8,128)(2,1)}, u32[]{:S(2)}, u32[]{:S(2)}) %all-to-all-start.1) | async-done | bytes 7340064 | tf_op jit(solution)/shard_map/all_to_all | solution.py:84
  490.4 10.1 %fusion.14 = bf16[1,224,4096]{2,1,0:T(8,128)(2,1)} fusion(bf16[32,28,4096]{2,1,0:T(8,128)(2,1)} %all-to-all-done.1, f32[32,28]{0,1:T(8,128)S(1)} %copy.31, f32[1,2,32,28,224]{4,2,3,1,0:T(8,128)S(1)} %bitcast_convert_fusion), kind=kOutput, calls=%fused_computation.16 | convolution fusion | flops 1646489600 | bytes 10784256 | tf_op jit(solution)/shard_map/escf,secw->efw/dot_general | solution.py:38
  500.5 2.5 all_gather.11
  503.1 5.7 fusion.32
  509.4 6.2 %fusion.30 = f32[32,28,224]{2,1,0:T(8,128)S(1)} fusion(bf16[32,28,4096]{2,1,0:T(8,128)(2,1)} %all-to-all-done.1, bf16[1,224,4096]{2,1,0:T(8,128)(2,1)} %all-gather.5.cloned.1.call-done), kind=kOutput, calls=%fused_computation.24 | convolution fusion | flops 1644167168 | bytes 9977856 | tf_op jit(solution)/shard_map/secw,efw->escf/dot_general | solution.py:37
  515.7 1.0 fusion.36
  516.7 30.8 %all-reduce = (f32[32,1,28]{0,2,1:T(8,128)S(1)}, f32[32,1,28]{0,2,1:T(8,128)S(1)}) all-reduce(f32[32,1,28]{0,2,1:T(8,128)S(1)} %bitcast.137, f32[32,1,28]{0,2,1:T(8,128)S(1)} %bitcast.136), channel_id=1, replica_groups=mesh['dp'=2,'expert'=32,'tensor'=8] {'tensor'}, use_global_device_ids=true, to_apply=%region_10.11 | all-reduce | flops 1792 | bytes 14336 | tf_op jit(solution)/shard_map/psum | solution.py:124
  548.2 7.1 %all-to-all-start.4 = ((f32[32,1,28]{2,1,0:T(1,128)}), f32[32,1,28]{2,1,0:T(1,128)S(1)}, u32[]{:S(2)}, u32[]{:S(2)}) async-start(f32[32,1,28]{2,1,0:T(1,128)} %copy.38), calls=%async_computation.6 | async-start | bytes 32768 | tf_op jit(solution)/shard_map/all_to_all | solution.py:129
  555.2 1.1 pad_maximum_fusion
  557.0 6.1 %all-to-all-done.4 = f32[32,1,28]{2,1,0:T(1,128)S(1)} async-done(((f32[32,1,28]{2,1,0:T(1,128)}), f32[32,1,28]{2,1,0:T(1,128)S(1)}, u32[]{:S(2)}, u32[]{:S(2)}) %all-to-all-start.4) | async-done | bytes 3616 | tf_op jit(solution)/shard_map/all_to_all | solution.py:129
  563.1 5.5 all-to-all-start.5
  568.7 0.9 pad_maximum_fusion.1
  570.8 5.9 all-to-all-done.5
  577.5 4.5 gather_fusion
  582.0 4.5 gather_fusion.1
  (60 shorter events, 10.8 us)
Async XLA Ops:
  8.0 63.4 %all-gather.3.cloned.1.call-start = ((), (), s32[]{:S(2)}) async-start(), calls=%async_computation.8 | async-start | bytes 1179648 | tf_op jit(solution)/shard_map/all_gather | solution.py:55
  39.5 21.7 %all-to-all-start = ((bf16[32,1,28]{2,1,0:T(2,128)(2,1)}), bf16[32,1,28]{2,1,0:T(2,128)(2,1)S(1)}, u32[]{:S(2)}, u32[]{:S(2)}) async-start(bf16[32,1,28]{2,1,0:T(2,128)(2,1)} %all_to_all.40), calls=%async_computation | async-start | bytes 32768 | tf_op jit(solution)/shard_map/all_to_all | solution.py:86
  61.3 35.1 %all-to-all-start.2 = ((bf16[32,1,28]{2,1,0:T(2,128)(2,1)}), bf16[32,1,28]{2,1,0:T(2,128)(2,1)S(1)}, u32[]{:S(2)}, u32[]{:S(2)}) async-start(bf16[32,1,28]{2,1,0:T(2,128)(2,1)} %all_to_all.41), calls=%async_computation.2 | async-start | bytes 32768 | tf_op jit(solution)/shard_map/all_to_all | solution.py:87
  96.3 10.4 %copy-start = (bf16[128,4096]{1,0:T(8,128)(2,1)S(1)}, bf16[128,4096]{1,0:T(8,128)(2,1)}, u32[]{:S(2)}) copy-start(bf16[128,4096]{1,0:T(8,128)(2,1)} %all-gather.3.cloned.1.call-done) | copy-start | bytes 3145732
  96.3 197.4 %all-to-all-start.3 = ((bf16[32,28,4096]{2,1,0:T(8,128)(2,1)}), bf16[32,28,4096]{2,1,0:T(8,128)(2,1)}, u32[]{:S(2)}, u32[]{:S(2)}) async-start(bf16[32,28,4096]{2,1,0:T(8,128)(2,1)} %reshape.389), calls=%async_computation.3 | async-start | bytes 16777216 | tf_op jit(solution)/shard_map/all_to_all | solution.py:85
  131.2 171.7 %copy-start.1 = (bf16[1,1,2,32,28,96]{5,3,4,2,1,0:T(8,128)(2,1)S(1)}, bf16[1,1,2,32,28,96]{5,3,4,2,1,0:T(8,128)(2,1)}, u32[]{:S(2)}) copy-start(bf16[1,1,2,32,28,96]{5,3,4,2,1,0:T(8,128)(2,1)} %param.13) | copy-start | bytes 1032196
  293.7 196.7 %all-to-all-start.1 = ((bf16[32,28,4096]{2,1,0:T(8,128)(2,1)}), bf16[32,28,4096]{2,1,0:T(8,128)(2,1)}, u32[]{:S(2)}, u32[]{:S(2)}) async-start(bf16[32,28,4096]{2,1,0:T(8,128)(2,1)} %reshape.387), calls=%async_computation.1 | async-start | bytes 16777216 | tf_op jit(solution)/shard_map/all_to_all | solution.py:84
  301.9 207.6 %all-gather.5.cloned.1.call-start = ((), (), s32[]{:S(2)}) async-start(), calls=%async_computation.9 | async-start | bytes 2752512 | tf_op jit(solution)/shard_map/all_gather | solution.py:90
  302.4 285.1 %reduce-scatter.5.cloned.1.call-start = ((), (), s32[]{:S(2)}) async-start(), calls=%async_computation.11 | async-start | bytes 1179648 | tf_op jit(solution)/shard_map/reduce_scatter | solution.py:120
  311.9 275.6 %reduce-scatter.3.cloned.1.call-start = ((), (), s32[]{:S(2)}) async-start(), calls=%async_computation.10 | async-start | bytes 2752512 | tf_op jit(solution)/shard_map/reduce_scatter | solution.py:117
  313.4 187.1 %copy-start.2 = (bf16[1,96,2048]{2,1,0:T(8,128)(2,1)S(1)}, bf16[1,96,2048]{2,1,0:T(8,128)(2,1)}, u32[]{:S(2)}) copy-start(bf16[1,96,2048]{2,1,0:T(8,128)(2,1)} %param.15) | copy-start | bytes 1179652
  548.2 14.9 %all-to-all-start.4 = ((f32[32,1,28]{2,1,0:T(1,128)}), f32[32,1,28]{2,1,0:T(1,128)S(1)}, u32[]{:S(2)}, u32[]{:S(2)}) async-start(f32[32,1,28]{2,1,0:T(1,128)} %copy.38), calls=%async_computation.6 | async-start | bytes 32768 | tf_op jit(solution)/shard_map/all_to_all | solution.py:129
  563.1 13.6 %all-to-all-start.5 = ((f32[32,1,28]{2,1,0:T(1,128)}), f32[32,1,28]{2,1,0:T(1,128)S(1)}, u32[]{:S(2)}, u32[]{:S(2)}) async-start(f32[32,1,28]{2,1,0:T(1,128)} %copy.39), calls=%async_computation.7 | async-start | bytes 32768 | tf_op jit(solution)/shard_map/all_to_all | solution.py:132
Sparse Core Ops, SparseCore 0:
  10.9 45.5 all-gather.2
Sparse Core Ops, SparseCore 1:
  304.4 19.2 all-gather.4
  326.9 17.6 reduce-scatter.4
  500.6 16.0 reduce-scatter.2
where the time goes:
time: 604 us; the launch traced here: 595 us
  waiting for transfers between devices  353 us (58%)
  local copies, waits for them, and re-layouts  80.3 us (13%)
  starting transfers between devices  55.1 us (9%)
  blocking collectives  33.4 us (6%)
  matrix products  30.8 us (5%)
  other arithmetic  26.9 us (4%)
  between operations  16.2 us (3%)
    all_to_all x1, waiting for transfers between devices, on_device(): lax.all_to_all(text_rows, 'expert', split_axis=0, concat_axis=0, tiled=True)  177 us
    all_to_all x1, waiting for transfers between devices, on_device(): lax.all_to_all(vision_rows, 'expert', split_axis=0, concat_axis=0, tiled=...  163 us
    psum x1, blocking collectives, on_device(): summed_scores = lax.psum((score_text, score_vision), 'tensor')  30.8 us
    dot_general x2, matrix products, family_piece(): jnp.einsum('escf,secw->efw', weighted, shaped, preferred_element_type=jnp...  18.8 us
    another operation x3, other arithmetic  18.2 us
    scatter x1, local copies, waits for them, and re-layouts, on_device(): vision_rows = blank_rows.at[vision_slot].set(spread, mode='drop').reshape...  16 us
    scatter x1, local copies, waits for them, and re-layouts, on_device(): blank_rows.at[text_slot].set(spread, mode='drop')  15.5 us
    all_to_all x1, starting transfers between devices, on_device(): lax.all_to_all(text_weight, 'expert', split_axis=0, concat_axis=0, tiled=...  13.4 us
  transfers between devices with their start and end apart: 10, of which 4 were waited for; matrix products, arithmetic and copies ran while one was open for 23% of the time, Pallas kernels for 0%

commit v1 on v0

v1 whole, which is shorter than its diff:
```python
import functools
import heapq

import jax
import jax.numpy as jnp
from jax import lax
from jax.experimental import pallas as pl
from jax.experimental.pallas import tpu as pltpu
from jax.sharding import PartitionSpec as P

MESH = pl.DeviceIdType.MESH
NL, NS, NT = 8, 4, 8
SLOT = 32
LINKS = ("l+", "l-", "s+", "s-")
SHIFT = {"l+": (0, -1), "l-": (0, 1), "s+": (-1, 0), "s-": (1, 0)}
SIZES = (1.0, 1.0, 1.0, 1.0, 0.125)


def hops(part, ds, dl, via):
    odd = part % 2
    right, left = (4, 3) if odd == 0 else (3, 4)
    up, down = (2, 1) if odd == 0 else (1, 2)
    out = []
    along_l = (via == "l+" and -dl < right) or (via == "l-" and dl < left)
    along_s = (via == "s+" and -ds < up) or (via == "s-" and ds < down)
    if part in (0, 1, 4):
        if dl == 0:
            if ds == 0:
                out += ["s+", "s-"]
            elif along_s:
                out.append(via)
            out += ["l+", "l-"]
        elif along_l:
            out.append(via)
    else:
        if ds == 0:
            if dl == 0:
                out += ["l+", "l-"]
            elif along_l:
                out.append(via)
            out += ["s+", "s-"]
        elif along_s:
            out.append(via)
    return out


def schedule():
    free = {link: 0.0 for link in LINKS}
    queue, count, log = [], 0, []
    for part in (4, 0, 2, 1, 3):
        heapq.heappush(queue, (0.0, count, part, 0, 0, None))
        count += 1
    while queue:
        now, _, part, ds, dl, via = heapq.heappop(queue)
        onward = hops(part, ds, dl, via)
        log.append((part, ds, dl, via, onward))
        for link in onward:
            free[link] = max(now, free[link]) + SIZES[part]
            step_s, step_l = SHIFT[link]
            item = (free[link] + 0.4, count, part, ds + step_s, dl + step_l, link)
            heapq.heappush(queue, item)
            count += 1
    return log


def half_of(t):
    return lax.rem((t + 1) // 2, 2)


def body(
    g_ref, meta_ref, wt_ref, wv_ref, pt_ref, pv_ref,
    gpt_ref, gpv_ref, gdt_ref, gdv_ref, sc_ref,
    buf, bufm, rows_t, rows_v, wtb, wvb, hid_t, hid_v, phid_t, phid_v,
    wgt_t, wgt_v, bown_t, bown_v, bsend_t, bsend_v, brecv_t, brecv_v,
    acc_t, acc_v, give_t, give_v, grecv_t, grecv_v, res_t, res_v,
    sel, sw, tmp_t, tmp_v,
    ysend, yrecv, csend, crecv, wsend, wrecv, hsend, hrecv, bsem, brsem,
    gsend, grsem, fsend, frecv,
):
    f32, bf16 = jnp.float32, jnp.bfloat16
    q = lax.axis_index("dp")
    e = lax.axis_index("expert")
    t = lax.axis_index("tensor")
    zl, xs = e // NS, lax.rem(e, NS)
    pair = t + 1 - 2 * lax.rem(t, 2)
    other = 1 - q
    mine = half_of(t)
    main = q == mine

    def chip(s_, l_):
        return lax.rem(l_ + 2 * NL, NL) * NS + lax.rem(s_ + 2 * NS, NS)

    near = {
        "l+": chip(xs, zl + 1), "l-": chip(xs, zl - 1),
        "s+": chip(xs + 1, zl), "s-": chip(xs - 1, zl),
    }

    barrier = pltpu.get_barrier_semaphore()
    for link in LINKS:
        pl.semaphore_signal(barrier, inc=1, device_id=(q, near[link], t), device_id_type=MESH)
    for k in range(1, NT):
        pl.semaphore_signal(
            barrier, inc=1, device_id=(q, e, lax.rem(t + k, NT)), device_id_type=MESH
        )
    pl.semaphore_signal(barrier, inc=1, device_id=(other, e, t), device_id_type=MESH)
    pl.semaphore_signal(barrier, inc=1, device_id=(other, e, pair), device_id_type=MESH)
    pl.semaphore_wait(barrier, 4 + NT - 1 + 2)

    def remote(src, dst, send, recv, where):
        return pltpu.make_async_remote_copy(
            src_ref=src, dst_ref=dst, send_sem=send, recv_sem=recv,
            device_id=where, device_id_type=MESH,
        )

    slice_id = lax.rem(t, 4)
    late = t // 4

    def taker(i):
        return (i // 2) * 4 + jnp.where(late == 0, 3 * (i % 2), 1 + (i % 2))

    for i in range(4):
        copy = remote(
            g_ref, buf.at[e, slice_id], ysend.at[i], yrecv.at[slice_id], (q, e, taker(i))
        )

        @pl.when(taker(i) != t)
        def _():
            copy.start()

        @pl.when(taker(i) == t)
        def _():
            pltpu.make_async_copy(g_ref, buf.at[e, slice_id], yrecv.at[slice_id]).start()

    keep = pltpu.make_async_copy(meta_ref, bufm.at[e], crecv.at[4, 0])
    keep.start()

    tmp_t[...] = jnp.zeros_like(tmp_t)
    tmp_v[...] = jnp.zeros_like(tmp_v)

    def pieces(ref, s):
        gate = ref[0, 0, 0, s].astype(f32)
        up = ref[0, 0, 1, s].astype(f32)
        sig = jax.nn.sigmoid(gate)
        return gate, up, sig

    def hidden_step(s, carry):
        for ref, tmp, hid in ((pt_ref, tmp_t, hid_t), (pv_ref, tmp_v, hid_v)):
            gate, up, sig = pieces(ref, s)
            tmp[0:28, :] = gate * sig * up
            hid[s] = tmp[...].astype(bf16)
        return carry

    lax.fori_loop(0, 32, hidden_step, 0)

    log = schedule()
    done_at = {}
    for n, (part, ds, dl, via, onward) in enumerate(log):
        dist = min(dl % NL, (-dl) % NL)
        done_at[dist] = n
    sent = {link: 0 for link in LINKS}
    sends = []
    later = []

    def at(part, src):
        return bufm.at[src] if part == 4 else buf.at[src, part]

    def early_sends():
        for k, (mine_ref, box) in enumerate(((hid_t, phid_t), (hid_v, phid_v))):
            copy = remote(mine_ref, box, hsend.at[k], hrecv.at[k], (q, e, pair))
            copy.start()
            later.append(copy)
        for k, (src, box) in enumerate(((wt_ref, wtb), (wv_ref, wvb))):
            @pl.when(main)
            def _():
                pltpu.make_async_copy(src.at[0], box.at[0], wrecv.at[0, k]).start()
                remote(
                    src.at[0], box.at[0], wsend.at[0, k], wrecv.at[0, k], (other, e, t)
                ).start()

            @pl.when(jnp.logical_not(main))
            def _():
                remote(
                    src.at[0], box.at[1], wsend.at[0, k], wrecv.at[1, k], (other, e, pair)
                ).start()
                remote(
                    src.at[0], box.at[1], wsend.at[1, k], wrecv.at[1, k], (q, e, pair)
                ).start()

    upper = (
        lax.broadcasted_iota(jnp.int32, (128, 128), 0)
        < lax.broadcasted_iota(jnp.int32, (128, 128), 1)
    ).astype(bf16)

    def block_of(dist, i):
        sign = 1 - 2 * (i // 4)
        return chip(xs + lax.rem(i, 4), zl + dist * sign)

    def gather_block(dist, i):
        src = block_of(dist, i)
        table = bufm[src].astype(f32)
        row = lax.broadcasted_iota(jnp.int32, (16, 512), 0)
        found = []
        for family in range(2):
            line = jnp.sum(
                jnp.where(row == family * 8 + e // 4, table, 0.0), axis=0, keepdims=True
            )
            w = jnp.zeros((1, 128), f32)
            for k in range(4):
                w = jnp.where(lax.rem(e, 4) == k, line[:, k * 128 : (k + 1) * 128], w)
            found.append(w)
        sub = lax.broadcasted_iota(jnp.int32, (8, 128), 0)
        both = jnp.where(sub == 0, found[0], jnp.where(sub == 1, found[1], 0.0))
        match = (both > 0.0).astype(bf16)
        rank = jnp.dot(match, upper, preferred_element_type=f32)
        want = lax.broadcasted_iota(jnp.int32, (SLOT, 128), 0).astype(f32)
        picks = []
        for family in range(2):
            w = found[family]
            hit = jnp.logical_and(want == rank[family : family + 1], w > 0.0)
            pick = jnp.where(hit, 1.0, 0.0)
            sw[family, src] = jnp.broadcast_to(
                jnp.sum(pick * w, axis=1, keepdims=True), (SLOT, 128)
            )
            picks.append(pick)
        pick = jnp.concatenate(picks, axis=0).astype(bf16)
        sel[src] = pick
        spot = pl.ds(pl.multiple_of(i * SLOT, SLOT), SLOT)
        for part in range(4):
            got = jnp.dot(pick, buf[src, part], preferred_element_type=f32).astype(bf16)
            cols = slice(part * 512, (part + 1) * 512)
            rows_t[spot, cols] = got[0:SLOT]
            rows_v[spot, cols] = got[SLOT : 2 * SLOT]
        for family, (wgt, own, their) in enumerate(
            ((wgt_t, hid_t, phid_t), (wgt_v, hid_v, phid_v))
        ):
            scale = sw[family, src][:, 0:1]
            wgt[0, spot] = (scale * own[src].astype(f32)).astype(bf16)
            wgt[1, spot] = (scale * their[src].astype(f32)).astype(bf16)

    start_of = {0: 0, 1: 128, 2: 384, 3: 640, 4: 896}
    families = (
        (rows_t, wtb, wgt_t, bown_t, bsend_t, brecv_t, acc_t),
        (rows_v, wvb, wgt_v, bown_v, bsend_v, brecv_v, acc_v),
    )

    def exchange(dist, k):
        m = 128 if dist in (0, 4) else 256
        rows = pl.ds(start_of[dist], m)
        fam = families[k]
        return remote(
            fam[4].at[rows], fam[5].at[rows], bsem.at[dist, k], brsem.at[dist, k], (q, e, pair)
        )

    def update(dist, part):
        m = 128 if dist in (0, 4) else 256
        cols = slice(part * 512, (part + 1) * 512)
        for rows, _, wgt, _, _, _, acc in families:
            for k in range(2):
                add = lax.dot_general(
                    wgt[k, 0:m], rows[0:m, cols], (((0,), (0,)), ((), ())),
                    preferred_element_type=f32,
                )
                if dist == 0:
                    acc[k, :, cols] = add
                else:
                    acc[k, :, cols] += add

    def work(dist):
        count = 4 if dist in (0, 4) else 8
        m = count * SLOT

        def step(i, carry):
            gather_block(dist, i)
            return carry

        lax.fori_loop(0, count, step, 0)
        base = start_of[dist]
        for k, (rows, wb, _, bown, bsend, _, _) in enumerate(families):
            nt = (((1,), (1,)), ((), ()))
            bsend[base : base + m] = lax.dot_general(
                rows[0:m], wb[1], nt, preferred_element_type=f32
            ).astype(bf16)
            exchange(dist, k).start()
        for k, (rows, wb, _, bown, bsend, _, _) in enumerate(families):
            nt = (((1,), (1,)), ((), ()))
            bown[base : base + m] = lax.dot_general(
                rows[0:m], wb[0], nt, preferred_element_type=f32
            )

    def finish(dist):
        count = 4 if dist in (0, 4) else 8
        for k in range(2):
            exchange(dist, k).wait()

        def step(i, carry):
            src = block_of(dist, i)
            spot = pl.ds(pl.multiple_of(start_of[dist] + i * SLOT, SLOT), SLOT)
            total = jnp.zeros((1, 128), f32)
            for family, (ref, out, bown, brecv) in enumerate(
                ((pt_ref, gpt_ref, bown_t, brecv_t), (pv_ref, gpv_ref, bown_v, brecv_v))
            ):
                back = (bown[spot] + brecv[spot].astype(f32))[0:28]
                gate, up, sig = pieces(ref, src)
                scaled = sw[family, src][0:28, 0:1] * back
                out[0, 0, 0, src] = (scaled * up * sig * (1.0 + gate * (1.0 - sig))).astype(bf16)
                out[0, 0, 1, src] = (scaled * gate * sig).astype(bf16)
                score = jnp.sum(gate * sig * up * back, axis=1, keepdims=True)
                pick = sel[src, family * SLOT : family * SLOT + SLOT].astype(f32)
                total += jnp.sum(pick[0:28] * score, axis=0, keepdims=True)
            sc_ref[pl.ds(src, 1), :] = total
            return carry

        lax.fori_loop(0, count, step, 0)

    waited_early = False
    for n, (part, ds, dl, via, onward) in enumerate(log):
        src = chip(xs + ds, zl + dl)
        if via is None:
            if part == 4:
                keep.wait()
            else:
                pltpu.make_async_copy(g_ref, buf.at[e, part], yrecv.at[part]).wait()
        else:
            here = at(part, src)
            pltpu.make_async_copy(here, here, crecv.at[part, (ds % NS) * NL + dl % NL]).wait()
        for link in onward:
            step_s, step_l = SHIFT[link]
            spot = ((ds + step_s) % NS) * NL + (dl + step_l) % NL
            copy = remote(
                at(part, src), at(part, src), csend.at[LINKS.index(link), sent[link]],
                crecv.at[part, spot], (q, near[link], t),
            )
            copy.start()
            sent[link] += 1
            sends.append(copy)
        if n == 4:
            early_sends()
        for dist in range(5):
            if done_at[dist] == n:
                if dist == 0:
                    for k, (mine_ref, box) in enumerate(((hid_t, phid_t), (hid_v, phid_v))):
                        later[k].wait_recv()
                    for k, (src_w, box) in enumerate(((wt_ref, wtb), (wv_ref, wvb))):
                        for slot in range(2):
                            pltpu.make_async_copy(
                                src_w.at[0], box.at[slot], wrecv.at[slot, k]
                            ).wait()
                work(dist)
                if dist < 4:
                    for part_ in range(4):
                        update(dist, part_)
                if dist > 0:
                    finish(dist - 1)

    chosen = jnp.where(main, 0, 1)
    given = 1 - chosen
    outs = ((acc_t, give_t, grecv_t, res_t, gdt_ref), (acc_v, give_v, grecv_v, res_v, gdv_ref))

    def hand(part, k):
        _, give, grecv, _, _ = outs[k]
        return remote(
            give.at[part], grecv.at[part], gsend.at[part, k], grsem.at[part, k], (other, e, t)
        )

    def forward(part, k):
        _, _, _, res, out = outs[k]
        cols = pl.ds(part * 512, 512)
        return remote(
            res.at[part], out.at[0, :, cols], fsend.at[part, k], frecv.at[part, k],
            (other, e, pair),
        )

    def add_up(part):
        cols = slice(part * 512, (part + 1) * 512)
        for k, (acc, give, grecv, res, out) in enumerate(outs):
            hand(part, k).wait_recv()
            here = acc[chosen, :, cols].astype(bf16).astype(f32)
            total = (here + grecv[part].astype(f32)).astype(bf16)

            @pl.when(main)
            def _():
                out[0, :, cols] = total

            @pl.when(jnp.logical_not(main))
            def _():
                res[part] = total
                forward(part, k).start()

    for part in range(4):
        update(4, part)
        cols = slice(part * 512, (part + 1) * 512)
        for k, (acc, give, grecv, res, out) in enumerate(outs):
            give[part] = acc[given, :, cols].astype(bf16)
            hand(part, k).start()
        if part > 0:
            add_up(part - 1)
    add_up(3)
    finish(4)

    for copy in sends:
        copy.wait_send()
    for copy in later:
        copy.wait_send()
    for part in range(4):
        for k in range(2):
            hand(part, k).wait_send()

            @pl.when(jnp.logical_not(main))
            def _():
                forward(part, k).wait()
    for k, (src, box) in enumerate(((wt_ref, wtb), (wv_ref, wvb))):
        pltpu.make_async_copy(src.at[0], box.at[0], wsend.at[0, k]).wait()

        @pl.when(jnp.logical_not(main))
        def _():
            pltpu.make_async_copy(src.at[0], box.at[0], wsend.at[1, k]).wait()

    for i in range(4):
        @pl.when(taker(i) != t)
        def _():
            pltpu.make_async_copy(g_ref, g_ref, ysend.at[i]).wait()


def owner_kernel(grad_out, meta, down_text, down_vision, pre_text, pre_vision):
    f32, bf16 = jnp.float32, jnp.bfloat16
    ft, fv = pre_text.shape[-1], pre_vision.shape[-1]
    vmem = pl.BlockSpec(memory_space=pltpu.VMEM)
    dma = pltpu.SemaphoreType.DMA
    like = jax.ShapeDtypeStruct
    return pl.pallas_call(
        body,
        out_shape=(
            like(pre_text.shape, bf16), like(pre_vision.shape, bf16),
            like(down_text.shape, bf16), like(down_vision.shape, bf16),
            like((32, 128), f32),
        ),
        in_specs=[vmem] * 6,
        out_specs=(vmem,) * 5,
        scratch_shapes=[
            pltpu.VMEM((32, 4, 128, 512), bf16), pltpu.VMEM((32, 16, 512), bf16),
            pltpu.VMEM((256, 2048), bf16), pltpu.VMEM((256, 2048), bf16),
            pltpu.VMEM((2, ft, 2048), bf16), pltpu.VMEM((2, fv, 2048), bf16),
            pltpu.VMEM((32, SLOT, ft), bf16), pltpu.VMEM((32, SLOT, fv), bf16),
            pltpu.VMEM((32, SLOT, ft), bf16), pltpu.VMEM((32, SLOT, fv), bf16),
            pltpu.VMEM((2, 256, ft), bf16), pltpu.VMEM((2, 256, fv), bf16),
            pltpu.VMEM((1024, ft), f32), pltpu.VMEM((1024, fv), f32),
            pltpu.VMEM((1024, ft), bf16), pltpu.VMEM((1024, fv), bf16),
            pltpu.VMEM((1024, ft), bf16), pltpu.VMEM((1024, fv), bf16),
            pltpu.VMEM((2, ft, 2048), f32), pltpu.VMEM((2, fv, 2048), f32),
            pltpu.VMEM((4, ft, 512), bf16), pltpu.VMEM((4, fv, 512), bf16),
            pltpu.VMEM((4, ft, 512), bf16), pltpu.VMEM((4, fv, 512), bf16),
            pltpu.VMEM((4, ft, 512), bf16), pltpu.VMEM((4, fv, 512), bf16),
            pltpu.VMEM((32, 2 * SLOT, 128), bf16), pltpu.VMEM((2, 32, SLOT, 128), f32),
            pltpu.VMEM((SLOT, ft), f32), pltpu.VMEM((SLOT, fv), f32),
            dma((4,)), dma((4,)), dma((4, 56)), dma((5, 32)),
            dma((2, 2)), dma((2, 2)), dma((2,)), dma((2,)), dma((5, 2)), dma((5, 2)),
            dma((4, 2)), dma((4, 2)), dma((4, 2)), dma((4, 2)),
        ],
        compiler_params=pltpu.CompilerParams(
            collective_id=0, has_side_effects=True, vmem_limit_bytes=60 * 1024 * 1024
        ),
        cost_estimate=pl.CostEstimate(
            flops=7_000_000_000, bytes_accessed=10_000_000, transcendentals=2_000_000
        ),
    )(grad_out, meta, down_text, down_vision, pre_text, pre_vision)


def on_device(grad_out, routes, probs, vision, pre_text, pre_vision, down_text, down_vision):
    experts = jnp.arange(32, dtype=jnp.int32)
    hit = routes[None, :, :] == experts[:, None, None]
    weight = jnp.sum(jnp.where(hit, probs[None].astype(jnp.float32), 0.0), axis=2)
    meta = jnp.concatenate(
        [jnp.where(vision == 0, weight, 0.0), jnp.where(vision == 1, weight, 0.0)], axis=0
    )
    meta = meta.astype(jnp.bfloat16).reshape(16, 512)
    gpt, gpv, gdt, gdv, score = owner_kernel(
        grad_out, meta, down_text, down_vision, pre_text, pre_vision
    )
    score = lax.psum(score, "tensor")
    back = lax.all_to_all(score, "expert", split_axis=0, concat_axis=0, tiled=True)
    grad_probs = jnp.sum(jnp.where(hit, back[:, :, None], 0.0), axis=0)
    return gpt, gpv, gdt, gdv, grad_probs


def solution(mesh):
    in_specs = (
        P(("dp", "expert"), "tensor"),
        P(("dp", "expert"), None),
        P(("dp", "expert"), None),
        P(("dp", "expert")),
        P("dp", "expert", None, None, None, "tensor"),
        P("dp", "expert", None, None, None, "tensor"),
        P("expert", "tensor", "dp"),
        P("expert", "tensor", "dp"),
    )
    out_specs = (
        P("dp", "expert", None, None, None, "tensor"),
        P("dp", "expert", None, None, None, "tensor"),
        P("expert", "tensor", "dp"),
        P("expert", "tensor", "dp"),
        P(("dp", "expert"), None),
    )
    return jax.shard_map(
        on_device, mesh=mesh, in_specs=in_specs, out_specs=out_specs, check_vma=False
    )
```

time: 604 us -> 228 us (0.38); the launches traced: 595 us -> 227 us
  waiting for transfers between devices: 353 us -> 4.21 us
  Pallas kernels: 0 us -> 155 us
  local copies, waits for them, and re-layouts: 80.3 us -> 9.77 us
  starting transfers between devices: 55.1 us -> 7.74 us
  matrix products: 30.8 us -> 0 us
  other arithmetic: 26.9 us -> 2.12 us
  between operations: 16.2 us -> 0.69 us
  blocking collectives: 33.4 us -> 47.5 us
    all_to_all x6 -> x1, waiting for transfers between devices: 352 us -> 4.21 us  [on_device(): lax.all_to_all(score, 'expert', split_axis=0, concat_axis=0, tiled=True)]
    pallas_call x0 -> x1, Pallas kernels: none -> 155 us  [owner_kernel(): pl.pallas_call(body, out_shape=(like(pre_text.shape, bf16), like(pre_visi...]
    all_to_all x6 -> x1, starting transfers between devices: 54.5 us -> 7.74 us  [on_device(): lax.all_to_all(score, 'expert', split_axis=0, concat_axis=0, tiled=True)]
    scatter x4 -> x0, local copies, waits for them, and re-layouts: 46.6 us -> none  [the longest x1 16 us: on_device(): vision_rows = blank_rows.at[vision_slot].set(spread, mode='drop').reshape...]
    dot_general x4 -> x0, matrix products: 30.8 us -> none  [the longest x2 18.8 us: family_piece(): jnp.einsum('escf,secw->efw', weighted, shaped, preferred_element_type=jnp...]
    another operation x7 -> x1, other arithmetic: 21.7 us -> 0.01 us
    reshape x5 -> x0, local copies, waits for them, and re-layouts: 18.2 us -> none  [the longest x1 8.99 us: on_device(): vision_rows = blank_rows.at[vision_slot].set(spread, mode='drop').reshape...]
    psum x1, blocking collectives: 30.8 us -> 47.5 us  [on_device(): score = lax.psum(score, 'tensor')]
  transfers between devices with their start and end apart: 10 -> 1, of which waited for: 4 -> 1; matrix products, arithmetic and copies ran while one was open for 23% -> 2% of each run, Pallas kernels for 0% -> 0%
where the time goes in v1:
time: 228 us; the launch traced here: 227 us
  Pallas kernels  155 us (68%)
  blocking collectives  47.5 us (21%)
  local copies, waits for them, and re-layouts  9.77 us (4%)
  starting transfers between devices  7.74 us (3%)
  waiting for transfers between devices  4.21 us (2%)
    pallas_call x1, Pallas kernels, owner_kernel(): pl.pallas_call(body, out_shape=(like(pre_text.shape, bf16), like(pre_visi...  155 us
    psum x1, blocking collectives, on_device(): score = lax.psum(score, 'tensor')  47.5 us
    unnamed x16, local copies, waits for them, and re-layouts  9.14 us
    all_to_all x1, starting transfers between devices, on_device(): lax.all_to_all(score, 'expert', split_axis=0, concat_axis=0, tiled=True)  7.74 us
  transfers between devices with their start and end apart: 1, of which 1 were waited for; matrix products, arithmetic and copies ran while one was open for 2% of the time, Pallas kernels for 0%

profile of v1, /device:TPU:6, one launch (start us, length us, event | category | flops | bytes accessed | tf_op | source)
XLA Modules:
  0.0 227.3 jit_solution(806920252365861649)
XLA Ops:
  0.6 0.0 copy-start.4
  0.6 0.0 copy-start.1
  0.7 0.7 broadcast_compare_fusion.1
  1.4 0.7 convert_element_type.9
  2.1 0.0 copy-done.4
  2.1 0.1 select_reduce_fusion.1
  2.2 0.6 convert_element_type.10.meta_ref
  2.8 2.0 copy.27.pv_ref
  4.8 0.0 copy-done.1
  4.8 1.5 copy.26.pt_ref
  6.3 155.3 %shard_map.119 = (bf16[1,1,2,32,28,224]{5,4,3,2,1,0:T(8,128)(2,1)}, bf16[1,1,2,32,28,96]{5,4,3,2,1,0:T(8,128)(2,1)}, bf16[1,224,2048]{2,1,0:T(8,128)(2,1)}, bf16[1,96,2048]{2,1,0:T(8,128)(2,1)}, f32[32,128]{1,0:T(8,128)}) custom-call(bf16[128,512]{1,0:T(8,128)(2,1)} %g_ref.1, bf16[16,512]{1,0:T(8,128)(2,1)} %convert_element_type.10.meta_ref, ...), custom_call_target="tpu_custom_call" | custom-call | flops 7000000000 | bytes 10000000 | tf_op jit(solution)/shard_map/pallas_call | solution.py:430
  161.6 47.5 %psum.7 = f32[32,1,128]{2,0,1:T(8,128)} all-reduce(f32[32,1,128]{2,0,1:T(8,128)} %bitcast.4), channel_id=1, replica_groups=mesh['dp'=2,'expert'=32,'tensor'=8] {'tensor'}, use_global_device_ids=true, to_apply=%region_1.2 | all-reduce | flops 4096 | bytes 32768 | tf_op jit(solution)/shard_map/psum | solution.py:479
  209.1 7.7 %all-to-all-start = ((f32[32,1,128]{2,1,0:T(1,128)}), f32[32,1,128]{2,1,0:T(1,128)S(1)}, u32[]{:S(2)}, u32[]{:S(2)}) async-start(f32[32,1,128]{2,1,0:T(1,128)} %bitcast.1), calls=%async_computation | async-start | bytes 32768 | tf_op jit(solution)/shard_map/all_to_all | solution.py:480
  216.8 0.0 copy-start.2
  216.8 2.7 %copy.29 = bf16[1,1,2,32,28,224]{5,3,4,2,1,0:T(8,128)(2,1)} copy(bf16[1,1,2,32,28,224]{5,4,3,2,1,0:T(8,128)(2,1)} %get-tuple-element.25) | data formatting | bytes 1605632
  219.5 0.0 copy-start
  219.5 0.0 copy-done.2
  219.5 0.9 copy.30
  220.5 4.2 %all-to-all-done = f32[32,1,128]{2,1,0:T(1,128)S(1)} async-done(((f32[32,1,128]{2,1,0:T(1,128)}), f32[32,1,128]{2,1,0:T(1,128)S(1)}, u32[]{:S(2)}, u32[]{:S(2)}) %all-to-all-start) | async-done | bytes 16416 | tf_op jit(solution)/shard_map/all_to_all | solution.py:480
  224.7 0.6 select_reduce_fusion
  225.3 0.0 copy-done
  225.3 0.0 copy-start.3
  225.3 0.9 copy.33
  226.2 0.3 copy-done.3
  226.5 0.7 copy.34
  (2 shorter events, 0.0 us)
Async XLA Ops:
  0.6 1.4 copy-start.4
  0.6 4.1 %copy-start.1 = (bf16[1,1,2,32,28,224]{5,3,4,2,1,0:T(8,128)(2,1)S(1)}, bf16[1,1,2,32,28,224]{5,3,4,2,1,0:T(8,128)(2,1)}, u32[]{:S(2)}) copy-start(bf16[1,1,2,32,28,224]{5,3,4,2,1,0:T(8,128)(2,1)} %param.12) | copy-start | bytes 2408452
  209.1 15.6 %all-to-all-start = ((f32[32,1,128]{2,1,0:T(1,128)}), f32[32,1,128]{2,1,0:T(1,128)S(1)}, u32[]{:S(2)}, u32[]{:S(2)}) async-start(f32[32,1,128]{2,1,0:T(1,128)} %bitcast.1), calls=%async_computation | async-start | bytes 32768 | tf_op jit(solution)/shard_map/all_to_all | solution.py:480
  216.8 2.7 %copy-start.2 = (bf16[1,1,2,32,28,96]{5,4,3,2,1,0:T(8,128)(2,1)S(1)}, bf16[1,1,2,32,28,96]{5,4,3,2,1,0:T(8,128)(2,1)}, u32[]{:S(2)}) copy-start(bf16[1,1,2,32,28,96]{5,4,3,2,1,0:T(8,128)(2,1)} %get-tuple-element.26) | copy-start | bytes 1032196
  219.5 5.8 %copy-start = (bf16[1,224,2048]{2,1,0:T(8,128)(2,1)S(1)}, bf16[1,224,2048]{2,1,0:T(8,128)(2,1)}, u32[]{:S(2)}) copy-start(bf16[1,224,2048]{2,1,0:T(8,128)(2,1)} %get-tuple-element.41) | copy-start | bytes 2752516
  225.3 1.2 copy-start.3

commit v2 on v0

v2 whole, which is shorter than its diff:
```python
import heapq

import jax
import jax.numpy as jnp
from jax import lax
from jax.experimental import pallas as pl
from jax.experimental.pallas import tpu as pltpu
from jax.sharding import PartitionSpec as P

MESH = pl.DeviceIdType.MESH
NL, NS, NT = 8, 4, 8
SLOT = 32
CAP = 28
LINKS = ("l+", "l-", "s+", "s-")
SHIFT = {"l+": (0, -1), "l-": (0, 1), "s+": (-1, 0), "s-": (1, 0)}
META = 3
CHUNKS = (
    (META, "s", 0, (0, 64), (0, 128), 0.0),
    (0, "s", 0, (0, 48), (0, 512), 0.0),
    (0, "l", 1, (48, 128), (0, 512), 0.0),
    (1, "s", 1, (0, 48), (0, 512), 3.0),
    (1, "l", 0, (48, 128), (0, 512), 3.0),
    (2, "s", 0, (0, 48), (0, 256), 4.5),
    (2, "s", 1, (0, 48), (256, 512), 4.5),
    (2, "l", 0, (48, 128), (0, 256), 4.5),
    (2, "l", 1, (48, 128), (256, 512), 4.5),
)
FIRST_TASK = 9.0
DELAY = 14
GROUPS = 5
BASE = {0: 0, 1: 128, 2: 384, 3: 640, 4: 896}
BLOCKS = {0: 4, 1: 8, 2: 8, 3: 8, 4: 4}


def hops(first, odd, ds, dl, via):
    right, left = (4, 3) if odd == 0 else (3, 4)
    up, down = (2, 1) if odd == 0 else (1, 2)
    out = []
    along_l = (via == "l+" and -dl < right) or (via == "l-" and dl < left)
    along_s = (via == "s+" and -ds < up) or (via == "s-" and ds < down)
    if first == "s":
        if dl == 0:
            if ds == 0:
                out += ["s+", "s-"]
            elif along_s:
                out.append(via)
            out += ["l+", "l-"]
        elif along_l:
            out.append(via)
    else:
        if ds == 0:
            if dl == 0:
                out += ["l+", "l-"]
            elif along_l:
                out.append(via)
            out += ["s+", "s-"]
        elif along_s:
            out.append(via)
    return out


def schedule():
    free = {link: 0.0 for link in LINKS}
    queue, count, log = [], 0, []
    for c, chunk in enumerate(CHUNKS):
        heapq.heappush(queue, (chunk[5], count, c, 0, 0, None))
        count += 1
    while queue:
        now, _, c, ds, dl, via = heapq.heappop(queue)
        _, first, odd, rows, cols, _ = CHUNKS[c]
        size = (rows[1] - rows[0]) * (cols[1] - cols[0]) / (128 * 512)
        onward = hops(first, odd, ds, dl, via)
        log.append((now, c, ds, dl, via, onward))
        for link in onward:
            free[link] = max(now, free[link]) + size
            step_s, step_l = SHIFT[link]
            item = (free[link] + 0.4, count, c, ds + step_s, dl + step_l, link)
            heapq.heappush(queue, item)
            count += 1
    return log


def slice_of(j, t):
    odd = lax.rem(t, 2)
    mate = lax.rem(t + NT + 2 * odd - 1, NT)
    if j == 0:
        return t
    if j == 1:
        return lax.rem(t + NT + 3 - 6 * odd, NT)
    if j == 2:
        return slice_of(1, mate)
    return mate


def body(
    g_ref, routes_ref, probs_ref, vision_ref, wt_ref, wv_ref, pt_ref, pv_ref,
    gpt_ref, gpv_ref, gdt_ref, gdv_ref, gp_ref,
    buf, bufm, rows_t, rows_v, srow_t, srow_v, prow_t, prow_v, wb_t, wb_v,
    wgt_t, wgt_v, pwgt_t, pwgt_v, bown_t, bown_v, bpair_t, bpair_v,
    bsend_t, bsend_v, brecv_t, brecv_v, acc_t, acc_v, give_t, give_v,
    grecv_t, grecv_v, res_t, res_v, sel, sw, tmp_t, tmp_v, scs, p1, scin, gall,
    ysend, yrecv, csend, crecv, wsend, wrecv, wback, hsend, hrecv, rsend, rrecv,
    bsem, brsem, gsend, grsem, fsend, frecv, s1send, s1recv, s2send, s2recv,
    tsend, trecv,
):
    f32, bf16 = jnp.float32, jnp.bfloat16
    q = lax.axis_index("dp")
    e = lax.axis_index("expert")
    t = lax.axis_index("tensor")
    zl, xs = e // NS, lax.rem(e, NS)
    pair = t + 1 - 2 * lax.rem(t, 2)
    mate = slice_of(3, t)
    far = slice_of(1, t)
    other = 1 - q

    def chip(s_, l_):
        return lax.rem(l_ + 2 * NL, NL) * NS + lax.rem(s_ + 2 * NS, NS)

    near = {
        "l+": chip(xs, zl + 1), "l-": chip(xs, zl - 1),
        "s+": chip(xs + 1, zl), "s-": chip(xs - 1, zl),
    }

    barrier = pltpu.get_barrier_semaphore()

    def greet(where):
        pl.semaphore_signal(barrier, inc=1, device_id=where, device_id_type=MESH)

    for k in range(1, NL):
        greet((q, chip(xs, zl + k), t))
    for k in range(1, NS):
        greet((q, chip(xs + k, zl), t))
    for k in range(1, NT):
        greet((q, e, lax.rem(t + k, NT)))
    greet((other, e, t))
    pl.semaphore_wait(barrier, NL + NS + NT - 3 + 1)

    def remote(src, dst, send, recv, where):
        return pltpu.make_async_remote_copy(
            src_ref=src, dst_ref=dst, send_sem=send, recv_sem=recv,
            device_id=where, device_id_type=MESH,
        )

    def arrived(ref, sem):
        pltpu.make_async_copy(ref, ref, sem).wait()

    y_copies = (
        remote(g_ref, buf.at[1, e], ysend.at[0], yrecv.at[0], (q, e, far)),
        remote(buf.at[1, e], buf.at[2, e], ysend.at[1], yrecv.at[1], (q, e, mate)),
    )
    y_copies[0].start()
    own = pltpu.make_async_copy(g_ref, buf.at[0, e], yrecv.at[2])
    own.start()

    expert = lax.broadcasted_iota(jnp.int32, (32, 128), 0)
    weight = jnp.zeros((32, 128), f32)
    for k in range(8):
        named = routes_ref[k : k + 1, :] == expert
        weight += jnp.where(named, probs_ref[k : k + 1, :], 0.0)
    image = vision_ref[...] == 1
    bufm[e, 0:32] = jnp.where(image, 0.0, weight).astype(bf16)
    bufm[e, 32:64] = jnp.where(image, weight, 0.0).astype(bf16)
    tmp_t[...] = jnp.zeros_like(tmp_t)
    tmp_v[...] = jnp.zeros_like(tmp_v)
    own.wait()

    w_fams = ((wt_ref, wb_t), (wv_ref, wb_v))

    def w_cols(u):
        return pl.ds(pl.multiple_of(lax.rem(u, 4) * 512, 512), 512)

    def w_copies(j, k, action):
        src, box = w_fams[k]
        u = slice_of(j, t)
        v = slice_of(j, pair)

        @pl.when(u // 4 == q)
        def _():
            here = src.at[0, :, w_cols(u)]
            there = remote(here, box.at[0, j], wsend.at[0, j, k], wrecv.at[0, j, k], (other, e, t))
            if action == "start":
                pltpu.make_async_copy(here, box.at[0, j], wrecv.at[0, j, k]).start()
                there.start()
            else:
                there.wait_send()

        @pl.when(v // 4 == q)
        def _():
            there = remote(
                src.at[0, :, w_cols(v)], box.at[1, j], wsend.at[1, j, k], wrecv.at[1, j, k],
                (q, e, pair),
            )
            if action == "start":
                there.start()
            else:
                there.wait_send()

    def w_relay(j, k):
        box = w_fams[k][1]
        return remote(
            box.at[1, j], box.at[1, j], wback.at[j, k], wrecv.at[1, j, k], (other, e, t)
        )

    def w_arrive():
        for j in range(4):
            for k in range(2):
                arrived(w_fams[k][1].at[1, j], wrecv.at[1, j, k])

                @pl.when(slice_of(j, t) // 4 == q)
                def _():
                    w_relay(j, k).start()

        for j in range(4):
            for k in range(2):
                arrived(w_fams[k][1].at[0, j], wrecv.at[0, j, k])

    def w_relayed():
        for j in range(4):
            for k in range(2):
                @pl.when(slice_of(j, t) // 4 == q)
                def _():
                    w_relay(j, k).wait_send()

    upper = (
        lax.broadcasted_iota(jnp.int32, (128, 128), 0)
        < lax.broadcasted_iota(jnp.int32, (128, 128), 1)
    ).astype(bf16)

    def block_of(g, i):
        sign = 1 - 2 * (i // 4)
        return chip(xs + lax.rem(i, 4), zl + g * sign)

    def place(g, i):
        return pl.ds(pl.multiple_of(BASE[g] + i * SLOT, SLOT), SLOT)

    def span(g):
        return slice(BASE[g], BASE[g] + BLOCKS[g] * SLOT)

    def pieces(ref, s):
        gate = ref[0, 0, 0, s].astype(f32)
        up = ref[0, 0, 1, s].astype(f32)
        return gate, up, jax.nn.sigmoid(gate)

    fams = (
        dict(pre=pt_ref, grad=gpt_ref, rows=rows_t, srow=srow_t, prow=prow_t, wb=wb_t, wgt=wgt_t,
             pwgt=pwgt_t, bown=bown_t, bpair=bpair_t, bsend=bsend_t, brecv=brecv_t, acc=acc_t,
             give=give_t, grecv=grecv_t, res=res_t, out=gdt_ref, tmp=tmp_t),
        dict(pre=pv_ref, grad=gpv_ref, rows=rows_v, srow=srow_v, prow=prow_v, wb=wb_v, wgt=wgt_v,
             pwgt=pwgt_v, bown=bown_v, bpair=bpair_v, bsend=bsend_v, brecv=brecv_v, acc=acc_v,
             give=give_v, grecv=grecv_v, res=res_v, out=gdv_ref, tmp=tmp_v),
    )

    def wgt_copy(g, k):
        at = pl.ds(BASE[g], BLOCKS[g] * SLOT)
        return remote(
            fams[k]["wgt"].at[at], fams[k]["pwgt"].at[at], hsend.at[g, k], hrecv.at[g, k],
            (q, e, pair),
        )

    def prepare(g):
        def step(i, carry):
            src = block_of(g, i)
            table = bufm[src].astype(f32)
            row = lax.broadcasted_iota(jnp.int32, (64, 128), 0)
            found = [
                jnp.sum(jnp.where(row == k * 32 + e, table, 0.0), axis=0, keepdims=True)
                for k in range(2)
            ]
            sub = lax.broadcasted_iota(jnp.int32, (8, 128), 0)
            both = jnp.where(sub == 0, found[0], jnp.where(sub == 1, found[1], 0.0))
            rank = jnp.dot((both > 0.0).astype(bf16), upper, preferred_element_type=f32)
            want = lax.broadcasted_iota(jnp.int32, (SLOT, 128), 0).astype(f32)
            for k, fam in enumerate(fams):
                hit = jnp.logical_and(want == rank[k : k + 1], found[k] > 0.0)
                pick = jnp.where(hit, 1.0, 0.0)
                scale = jnp.sum(pick * found[k], axis=1, keepdims=True)
                sw[k, src] = jnp.broadcast_to(scale, (SLOT, 128))
                sel[src, k * SLOT : (k + 1) * SLOT] = pick.astype(bf16)
                gate, up, sig = pieces(fam["pre"], src)
                fam["tmp"][0:CAP, :] = gate * sig * up
                fam["wgt"][place(g, i)] = (scale * fam["tmp"][...]).astype(bf16)
            return carry

        lax.fori_loop(0, BLOCKS[g], step, 0)
        for k in range(2):
            wgt_copy(g, k).start()

    def row_copy(g, k):
        at = pl.ds(BASE[g], BLOCKS[g] * SLOT)
        return remote(
            fams[k]["srow"].at[at], fams[k]["prow"].at[at], rsend.at[g, k], rrecv.at[g, k],
            (q, e, mate),
        )

    def back_copy(g, k):
        at = pl.ds(BASE[g], BLOCKS[g] * SLOT)
        return remote(
            fams[k]["bsend"].at[at], fams[k]["brecv"].at[at], bsem.at[g, k], brsem.at[g, k],
            (q, e, pair),
        )

    nt_dims = (((1,), (1,)), ((), ()))
    tn_dims = (((0,), (0,)), ((), ()))
    waited = set()
    begun = set()
    added = {g: 0 for g in range(GROUPS)}

    def select(j, g):
        def step(i, carry):
            src = block_of(g, i)
            got = jnp.dot(sel[src], buf[j, src], preferred_element_type=f32).astype(bf16)
            for k, fam in enumerate(fams):
                if j == 0:
                    fam["srow"][place(g, i)] = got[k * SLOT : (k + 1) * SLOT]
                else:
                    spot = pl.ds(pl.multiple_of(i * SLOT, SLOT), SLOT)
                    fam["rows"][spot] = got[k * SLOT : (k + 1) * SLOT]
            return carry

        lax.fori_loop(0, BLOCKS[g], step, 0)
        if j == 0:
            for k in range(2):
                row_copy(g, k).start()

    def products(j, g):
        m = BLOCKS[g] * SLOT
        if g not in waited:
            waited.add(g)
            for k in range(2):
                wgt_copy(g, k).wait_recv()
        if j == 3:
            for k in range(2):
                row_copy(g, k).wait_recv()
        final = added[g] == 3
        for k, fam in enumerate(fams):
            rows = {0: fam["srow"], 3: fam["prow"]}.get(j)
            rows = fam["rows"][0:m] if rows is None else rows[span(g)]
            theirs = lax.dot_general(rows, fam["wb"][1, j], nt_dims, preferred_element_type=f32)
            if added[g]:
                theirs += fam["bpair"][span(g)]
            if final:
                fam["bsend"][span(g)] = theirs.astype(bf16)
                back_copy(g, k).start()
            else:
                fam["bpair"][span(g)] = theirs
        for k, fam in enumerate(fams):
            rows = {0: fam["srow"], 3: fam["prow"]}.get(j)
            rows = fam["rows"][0:m] if rows is None else rows[span(g)]
            ours = lax.dot_general(rows, fam["wb"][0, j], nt_dims, preferred_element_type=f32)
            if added[g]:
                ours += fam["bown"][span(g)]
            fam["bown"][span(g)] = ours
            for n, wgt in enumerate((fam["wgt"], fam["pwgt"])):
                add = lax.dot_general(wgt[span(g)], rows, tn_dims, preferred_element_type=f32)
                if j in begun:
                    fam["acc"][n, j] += add
                else:
                    fam["acc"][n, j] = add
        added[g] += 1
        begun.add(j)
        return final

    def hand(j, k):
        fam = fams[k]
        return remote(
            fam["give"].at[j], fam["grecv"].at[j], gsend.at[j, k], grsem.at[j, k], (other, e, t)
        )

    def forward(j, k):
        fam = fams[k]
        return remote(
            fam["res"].at[j], fam["out"].at[0, :, w_cols(slice_of(j, t))], fsend.at[j, k],
            frecv.at[j, k], (q, e, pair),
        )

    def give_away(j):
        @pl.when(slice_of(j, t) // 4 != q)
        def _():
            for k, fam in enumerate(fams):
                fam["give"][j] = fam["acc"][:, j].astype(bf16)
                hand(j, k).start()

    def add_up(j):
        @pl.when(slice_of(j, t) // 4 == q)
        def _():
            for k, fam in enumerate(fams):
                hand(j, k).wait_recv()
                for n in (1, 0):
                    here = fam["acc"][n, j].astype(bf16).astype(f32)
                    total = (here + fam["grecv"][j, n].astype(f32)).astype(bf16)
                    if n == 1:
                        fam["res"][j] = total
                        forward(j, k).start()
                    else:
                        fam["out"][0, :, w_cols(slice_of(j, t))] = total

    def score_copy(g, sign):
        to = lax.rem(zl + sign * g + NL, NL)
        return remote(
            scs.at[pl.ds(to * NS, NS)], p1.at[:, zl], s1send.at[(sign * g) % NL],
            s1recv.at[(-sign * g) % NL], (q, chip(xs, zl + sign * g), t),
        )

    def finish(g):
        for k in range(2):
            back_copy(g, k).wait_recv()

        def step(i, carry):
            src = block_of(g, i)
            total = jnp.zeros((1, 128), f32)
            for k, fam in enumerate(fams):
                spot = place(g, i)
                back = (fam["bown"][spot] + fam["brecv"][spot].astype(f32))[0:CAP]
                gate, up, sig = pieces(fam["pre"], src)
                scaled = sw[k, src][0:CAP, 0:1] * back
                grad = fam["grad"]
                grad[0, 0, 0, src] = (scaled * up * sig * (1.0 + gate * (1.0 - sig))).astype(bf16)
                grad[0, 0, 1, src] = (scaled * gate * sig).astype(bf16)
                score = jnp.sum(gate * sig * up * back, axis=1, keepdims=True)
                pick = sel[src, k * SLOT : (k + 1) * SLOT].astype(f32)
                total += jnp.sum(pick[0:CAP] * score, axis=0, keepdims=True)
            scs[src] = total
            return carry

        lax.fori_loop(0, BLOCKS[g], step, 0)
        if g == 0:
            p1[:, zl] = scs[pl.ds(zl * NS, NS)]
        elif g == 4:
            score_copy(4, 1).start()
        else:
            score_copy(g, 1).start()
            score_copy(g, -1).start()

    log = schedule()
    ready = {}
    for n, (now, c, ds, dl, via, onward) in enumerate(log):
        ready[(CHUNKS[c][0], min(dl % NL, -dl % NL))] = n
    sent = {link: 0 for link in LINKS}
    sends = []
    todo = []
    groups_left = {j: GROUPS for j in range(4)}

    def plan(n, needs, call):
        todo.append((n, len(todo) + planned[0], needs, call))
        planned[0] += 1
        todo.sort(key=lambda item: item[:2])

    planned = [0]

    def multiply(n, j, g):
        if products(j, g):
            plan(n + DELAY, False, lambda m: finish(g))
        groups_left[j] -= 1
        if groups_left[j] == 0:
            give_away(j)
            plan(n + DELAY, False, lambda m: add_up(j))

    def first_rows(n, g):
        select(0, g)
        plan(n + DELAY, True, lambda m: multiply(m, 0, g))
        plan(n + 3 * DELAY, True, lambda m: multiply(m, 3, g))

    def more_rows(n, j, g):
        select(j, g)
        multiply(n, j, g)

    for g in range(GROUPS):
        plan(ready[(0, g)], False, lambda m, g=g: first_rows(m, g))
        for j in (1, 2):
            plan(ready[(j, g)], True, lambda m, j=j, g=g: more_rows(m, j, g))

    def run_one(n, anything=False):
        for spot, (least, _, needs, call) in enumerate(todo):
            if anything or (least <= n and (opened or not needs)):
                todo.pop(spot)
                call(n)
                return

    prepared = 0
    opened = False
    y_waited = set()
    for n, (now, c, ds, dl, via, onward) in enumerate(log):
        part, _, _, rows, cols, _ = CHUNKS[c]
        src = chip(xs + ds, zl + dl)
        if part == META:
            here = bufm.at[src]
        else:
            here = buf.at[part, src, rows[0] : rows[1], cols[0] : cols[1]]
        origin = here
        if via is None:
            if part == 0:
                origin = g_ref.at[rows[0] : rows[1], cols[0] : cols[1]]
            elif part != META and part not in y_waited:
                y_waited.add(part)
                arrived(buf.at[part, e], yrecv.at[part - 1])
                if part == 1:
                    y_copies[1].start()
        else:
            arrived(here, crecv.at[c, (ds % NS) * NL + dl % NL])
        for link in onward:
            step_s, step_l = SHIFT[link]
            spot = ((ds + step_s) % NS) * NL + (dl + step_l) % NL
            copy = remote(
                origin, here, csend.at[LINKS.index(link), sent[link]], crecv.at[c, spot],
                (q, near[link], t),
            )
            copy.start()
            sent[link] += 1
            sends.append(copy)
        if n == 2:
            for j in range(4):
                for k in range(2):
                    w_copies(j, k, "start")
        while prepared < GROUPS and ready[(META, prepared)] <= n:
            prepare(prepared)
            prepared += 1
        if not opened and now >= FIRST_TASK:
            opened = True
            w_arrive()
        run_one(n)
    while todo:
        run_one(len(log), True)

    for k in range(1, NL):
        arrived(p1.at[:, 0], s1recv.at[k])
    line = []
    for k in range(1, NS):
        to = lax.rem(xs + k, NS)
        copy = remote(
            p1.at[to], scin.at[xs], s2send.at[k - 1], s2recv.at[k - 1], (q, chip(xs + k, zl), t)
        )
        copy.start()
        line.append(copy)
    scin[xs] = p1[xs]
    for copy in line:
        copy.wait_recv()
    chosen = jnp.zeros((8, 128), f32)
    for owner in range(32):
        value = scin[owner % NS, owner // NS]
        chosen += jnp.where(routes_ref[...] == owner, value, 0.0)
    gall[t] = chosen
    for k in range(1, NT):
        copy = remote(
            gall.at[t], gall.at[t], tsend.at[k - 1], trecv.at[k - 1], (q, e, lax.rem(t + k, NT))
        )
        copy.start()
        line.append(copy)
    for copy in line[NS - 1 :]:
        copy.wait_recv()
    total = gall[0]
    for k in range(1, NT):
        total += gall[k]
    gp_ref[...] = total

    for copy in line:
        copy.wait_send()
    for copy in sends:
        copy.wait_send()
    for copy in y_copies:
        copy.wait_send()
    for j in range(4):
        for k in range(2):
            w_copies(j, k, "wait")
    w_relayed()
    for g in range(GROUPS):
        for k in range(2):
            wgt_copy(g, k).wait_send()
            row_copy(g, k).wait_send()
            back_copy(g, k).wait_send()
        if g == 4:
            score_copy(4, 1).wait_send()
        elif g > 0:
            score_copy(g, 1).wait_send()
            score_copy(g, -1).wait_send()
    for j in range(4):
        for k in range(2):
            @pl.when(slice_of(j, t) // 4 != q)
            def _():
                hand(j, k).wait_send()

            @pl.when(slice_of(j, t) // 4 == q)
            def _():
                forward(j, k).wait_send()

            @pl.when(slice_of(j, pair) // 4 == q)
            def _():
                arrived(fams[k]["res"].at[j], frecv.at[j, k])


def owner_kernel(grad_out, routes, probs, vision, down_text, down_vision, pre_text, pre_vision):
    f32, bf16 = jnp.float32, jnp.bfloat16
    ft, fv = pre_text.shape[-1], pre_vision.shape[-1]
    vmem = pl.BlockSpec(memory_space=pltpu.VMEM)
    dma = pltpu.SemaphoreType.DMA
    like = jax.ShapeDtypeStruct

    def two(shape, kind):
        return [pltpu.VMEM(shape(f), kind) for f in (ft, fv)]

    return pl.pallas_call(
        body,
        out_shape=(
            like(pre_text.shape, bf16), like(pre_vision.shape, bf16),
            like(down_text.shape, bf16), like(down_vision.shape, bf16),
            like((8, 128), f32),
        ),
        in_specs=[vmem] * 8,
        out_specs=(vmem,) * 5,
        scratch_shapes=[
            pltpu.VMEM((3, 32, 128, 512), bf16), pltpu.VMEM((32, 64, 128), bf16),
            *two(lambda f: (256, 512), bf16), *two(lambda f: (1024, 512), bf16),
            *two(lambda f: (1024, 512), bf16), *two(lambda f: (2, 4, f, 512), bf16),
            *two(lambda f: (1024, f), bf16), *two(lambda f: (1024, f), bf16),
            *two(lambda f: (1024, f), f32), *two(lambda f: (1024, f), f32),
            *two(lambda f: (1024, f), bf16), *two(lambda f: (1024, f), bf16),
            *two(lambda f: (2, 4, f, 512), f32), *two(lambda f: (4, 2, f, 512), bf16),
            *two(lambda f: (4, 2, f, 512), bf16), *two(lambda f: (4, f, 512), bf16),
            pltpu.VMEM((32, 2 * SLOT, 128), bf16), pltpu.VMEM((2, 32, SLOT, 128), f32),
            *two(lambda f: (SLOT, f), f32),
            pltpu.VMEM((32, 1, 128), f32), pltpu.VMEM((NS, NL, 1, 128), f32),
            pltpu.VMEM((NS, NL, 1, 128), f32), pltpu.VMEM((NT, 8, 128), f32),
            dma((2,)), dma((3,)), dma((4, 96)), dma((len(CHUNKS), 32)),
            dma((2, 4, 2)), dma((2, 4, 2)), dma((4, 2)),
            dma((5, 2)), dma((5, 2)), dma((5, 2)), dma((5, 2)), dma((5, 2)), dma((5, 2)),
            dma((4, 2)), dma((4, 2)), dma((4, 2)), dma((4, 2)),
            dma((NL,)), dma((NL,)), dma((NS - 1,)), dma((NS - 1,)),
            dma((NT - 1,)), dma((NT - 1,)),
        ],
        compiler_params=pltpu.CompilerParams(
            collective_id=0, has_side_effects=True, vmem_limit_bytes=60 * 1024 * 1024
        ),
        cost_estimate=pl.CostEstimate(
            flops=7_000_000_000, bytes_accessed=10_000_000, transcendentals=2_000_000
        ),
    )(grad_out, routes, probs, vision, down_text, down_vision, pre_text, pre_vision)


def on_device(grad_out, routes, probs, vision, pre_text, pre_vision, down_text, down_vision):
    gpt, gpv, gdt, gdv, gp = owner_kernel(
        grad_out, routes.T, probs.T.astype(jnp.float32), vision[None, :],
        down_text, down_vision, pre_text, pre_vision,
    )
    return gpt, gpv, gdt, gdv, gp.T


def solution(mesh):
    in_specs = (
        P(("dp", "expert"), "tensor"),
        P(("dp", "expert"), None),
        P(("dp", "expert"), None),
        P(("dp", "expert")),
        P("dp", "expert", None, None, None, "tensor"),
        P("dp", "expert", None, None, None, "tensor"),
        P("expert", "tensor", "dp"),
        P("expert", "tensor", "dp"),
    )
    out_specs = (
        P("dp", "expert", None, None, None, "tensor"),
        P("dp", "expert", None, None, None, "tensor"),
        P("expert", "tensor", "dp"),
        P("expert", "tensor", "dp"),
        P(("dp", "expert"), None),
    )
    return jax.shard_map(
        on_device, mesh=mesh, in_specs=in_specs, out_specs=out_specs, check_vma=False
    )
```

time: 604 us -> 144 us (0.24); the launches traced: 595 us -> 143 us
  waiting for transfers between devices: 353 us -> 0 us
  Pallas kernels: 0 us -> 131 us
  local copies, waits for them, and re-layouts: 80.3 us -> 10.1 us
  starting transfers between devices: 55.1 us -> 0 us
  blocking collectives: 33.4 us -> 0 us
  matrix products: 30.8 us -> 0 us
  other arithmetic: 26.9 us -> 1.36 us
  between operations: 16.2 us -> 0.66 us
    all_to_all x6 -> x0, waiting for transfers between devices: 352 us -> none  [the longest x1 177 us: on_device(): lax.all_to_all(text_rows, 'expert', split_axis=0, concat_axis=0, tiled=True)]
    pallas_call x0 -> x1, Pallas kernels: none -> 131 us  [owner_kernel(): pl.pallas_call(body, out_shape=(like(pre_text.shape, bf16), like(pre_visi...]
    all_to_all x6 -> x0, starting transfers between devices: 54.5 us -> none  [the longest x1 13.4 us: on_device(): lax.all_to_all(text_weight, 'expert', split_axis=0, concat_axis=0, tiled=...]
    scatter x4 -> x0, local copies, waits for them, and re-layouts: 46.6 us -> none  [the longest x1 16 us: on_device(): vision_rows = blank_rows.at[vision_slot].set(spread, mode='drop').reshape...]
    psum x1 -> x0, blocking collectives: 30.8 us -> none  [on_device(): summed_scores = lax.psum((score_text, score_vision), 'tensor')]
    dot_general x4 -> x0, matrix products: 30.8 us -> none  [the longest x2 18.8 us: family_piece(): jnp.einsum('escf,secw->efw', weighted, shaped, preferred_element_type=jnp...]
    another operation x7 -> x0, other arithmetic: 21.7 us -> none
    reshape x5 -> x0, local copies, waits for them, and re-layouts: 18.2 us -> none  [the longest x1 8.99 us: on_device(): vision_rows = blank_rows.at[vision_slot].set(spread, mode='drop').reshape...]
  transfers between devices with their start and end apart: 10 -> 0, of which waited for: 4 -> 0; matrix products, arithmetic and copies ran while one was open for 23% -> 0% of each run, Pallas kernels for 0% -> 0%
where the time goes in v2:
time: 144 us; the launch traced here: 143 us
  Pallas kernels  131 us (91%)
  local copies, waits for them, and re-layouts  10.1 us (7%)
    pallas_call x1, Pallas kernels, owner_kernel(): pl.pallas_call(body, out_shape=(like(pre_text.shape, bf16), like(pre_visi...  131 us
    unnamed x17, local copies, waits for them, and re-layouts  10.1 us

profile of v2, /device:TPU:6, one launch (start us, length us, event | category | flops | bytes accessed | tf_op | source)
XLA Modules:
  0.0 143.3 jit_solution(11611258512911300443)
XLA Ops:
  0.6 0.0 copy-start.1
  0.6 1.4 convert_bitcast_fusion.probs_ref
  2.0 2.0 %copy.14.pv_ref = bf16[1,1,2,32,28,96]{5,4,3,2,1,0:T(8,128)(2,1)} copy(bf16[1,1,2,32,28,96]{5,3,4,2,1,0:T(8,128)(2,1)} %param.13) | data formatting | bytes 688128 | tf_op args[5]
  4.0 0.0 copy-done.1
  4.0 1.5 %copy.13.pt_ref = bf16[1,1,2,32,28,224]{5,4,3,2,1,0:T(8,128)(2,1)} copy(bf16[1,1,2,32,28,224]{5,3,4,2,1,0:T(8,128)(2,1)S(1)} %copy-done.1) | data formatting | bytes 1605632 | tf_op args[4]
  5.5 131.2 %shard_map.119 = (bf16[1,1,2,32,28,224]{5,4,3,2,1,0:T(8,128)(2,1)}, bf16[1,1,2,32,28,96]{5,4,3,2,1,0:T(8,128)(2,1)}, bf16[1,224,2048]{2,1,0:T(8,128)(2,1)}, bf16[1,96,2048]{2,1,0:T(8,128)(2,1)}, f32[8,128]{1,0:T(8,128)}) custom-call(bf16[128,512]{1,0:T(8,128)(2,1)} %g_ref.1, s32[8,128]{1,0:T(8,128)} %bitcast.6, f32[8,128]{1,0:T(8,128)} %convert_bitcast_fusion.probs_ref, ...), custom_call_target="tpu_custom_call" | custom-call | flops 7000000000 | bytes 10000000 | tf_op jit(solution)/shard_map/pallas_call | solution.py:600
  136.7 0.0 copy-start.2
  136.7 2.7 %copy.15 = bf16[1,1,2,32,28,224]{5,3,4,2,1,0:T(8,128)(2,1)} copy(bf16[1,1,2,32,28,224]{5,4,3,2,1,0:T(8,128)(2,1)} %get-tuple-element.15) | data formatting | bytes 1605632
  139.4 0.0 copy-done.2
  139.4 0.0 copy-start
  139.4 0.9 copy.16
  140.4 0.4 copy-done
  140.8 0.0 copy-start.3
  140.8 0.9 copy.20
  141.7 0.3 copy-done.3
  142.0 0.0 copy-start.4
  142.0 0.7 copy.21
  142.8 0.0 copy-done.4
  142.8 0.6 copy.22
Async XLA Ops:
  0.6 3.4 %copy-start.1 = (bf16[1,1,2,32,28,224]{5,3,4,2,1,0:T(8,128)(2,1)S(1)}, bf16[1,1,2,32,28,224]{5,3,4,2,1,0:T(8,128)(2,1)}, u32[]{:S(2)}) copy-start(bf16[1,1,2,32,28,224]{5,3,4,2,1,0:T(8,128)(2,1)} %param.12) | copy-start | bytes 2408452
  136.7 2.7 %copy-start.2 = (bf16[1,1,2,32,28,96]{5,4,3,2,1,0:T(8,128)(2,1)S(1)}, bf16[1,1,2,32,28,96]{5,4,3,2,1,0:T(8,128)(2,1)}, u32[]{:S(2)}) copy-start(bf16[1,1,2,32,28,96]{5,4,3,2,1,0:T(8,128)(2,1)} %get-tuple-element.16) | copy-start | bytes 1032196
  139.4 1.3 copy-start
  140.8 1.2 copy-start.3
  142.0 0.8 copy-start.4

commit v3 on v2

--- a/solution.py
+++ b/solution.py
@@ -27,6 +27,8 @@
 )
 FIRST_TASK = 9.0
 DELAY = 14
+ROW_DELAY = 42
+W_STEP = 4
 GROUPS = 5
 BASE = {0: 0, 1: 128, 2: 384, 3: 640, 4: 896}
 BLOCKS = {0: 4, 1: 8, 2: 8, 3: 8, 4: 4}
@@ -154,9 +156,10 @@
 
     expert = lax.broadcasted_iota(jnp.int32, (32, 128), 0)
     weight = jnp.zeros((32, 128), f32)
+    probs = probs_ref[...].astype(f32)
     for k in range(8):
         named = routes_ref[k : k + 1, :] == expert
-        weight += jnp.where(named, probs_ref[k : k + 1, :], 0.0)
+        weight += jnp.where(named, probs[k : k + 1, :], 0.0)
     image = vision_ref[...] == 1
     bufm[e, 0:32] = jnp.where(image, 0.0, weight).astype(bf16)
     bufm[e, 32:64] = jnp.where(image, weight, 0.0).astype(bf16)
@@ -310,17 +313,21 @@
             src = block_of(g, i)
             got = jnp.dot(sel[src], buf[j, src], preferred_element_type=f32).astype(bf16)
             for k, fam in enumerate(fams):
-                if j == 0:
-                    fam["srow"][place(g, i)] = got[k * SLOT : (k + 1) * SLOT]
-                else:
-                    spot = pl.ds(pl.multiple_of(i * SLOT, SLOT), SLOT)
-                    fam["rows"][spot] = got[k * SLOT : (k + 1) * SLOT]
+                spot = pl.ds(pl.multiple_of(i * SLOT, SLOT), SLOT)
+                fam["rows"][spot] = got[k * SLOT : (k + 1) * SLOT]
             return carry
 
         lax.fori_loop(0, BLOCKS[g], step, 0)
-        if j == 0:
-            for k in range(2):
-                row_copy(g, k).start()
+
+    def select_shared(g, i):
+        got = jnp.dot(sel[block_of(g, i)], buf[0, block_of(g, i)], preferred_element_type=f32)
+        at = pl.ds(BASE[g] + i * SLOT, SLOT)
+        for k, fam in enumerate(fams):
+            fam["srow"][at] = got[k * SLOT : (k + 1) * SLOT].astype(bf16)
+            remote(
+                fam["srow"].at[at], fam["prow"].at[at], rsend.at[g, k], rrecv.at[g, k],
+                (q, e, mate),
+            ).start()
 
     def products(j, g):
         m = BLOCKS[g] * SLOT
@@ -432,9 +439,11 @@
             score_copy(g, -1).start()
 
     log = schedule()
-    ready = {}
+    ready, block_ready = {}, {}
     for n, (now, c, ds, dl, via, onward) in enumerate(log):
         ready[(CHUNKS[c][0], min(dl % NL, -dl % NL))] = n
+        if CHUNKS[c][0] == 0:
+            block_ready[(ds % NS, dl % NL)] = n
     sent = {link: 0 for link in LINKS}
     sends = []
     todo = []
@@ -455,17 +464,24 @@
             give_away(j)
             plan(n + DELAY, False, lambda m: add_up(j))
 
-    def first_rows(n, g):
-        select(0, g)
-        plan(n + DELAY, True, lambda m: multiply(m, 0, g))
-        plan(n + 3 * DELAY, True, lambda m: multiply(m, 3, g))
+    blocks_left = dict(BLOCKS)
+
+    def first_rows(n, g, i):
+        select_shared(g, i)
+        blocks_left[g] -= 1
+        if blocks_left[g] == 0:
+            plan(n + DELAY, True, lambda m: multiply(m, 0, g))
+            plan(n + ROW_DELAY, True, lambda m: multiply(m, 3, g))
 
     def more_rows(n, j, g):
         select(j, g)
         multiply(n, j, g)
 
     for g in range(GROUPS):
-        plan(ready[(0, g)], False, lambda m, g=g: first_rows(m, g))
+        for i in range(BLOCKS[g]):
+            dl = g if i < 4 else -g
+            least = max(block_ready[(i % 4, dl % NL)], ready[(META, g)])
+            plan(least, False, lambda m, g=g, i=i: first_rows(m, g, i))
         for j in (1, 2):
             plan(ready[(j, g)], True, lambda m, j=j, g=g: more_rows(m, j, g))
 
@@ -479,6 +495,7 @@
     prepared = 0
     opened = False
     y_waited = set()
+    w_begun = 0
     for n, (now, c, ds, dl, via, onward) in enumerate(log):
         part, _, _, rows, cols, _ = CHUNKS[c]
         src = chip(xs + ds, zl + dl)
@@ -507,10 +524,9 @@
             copy.start()
             sent[link] += 1
             sends.append(copy)
-        if n == 2:
-            for j in range(4):
-                for k in range(2):
-                    w_copies(j, k, "start")
+        if n >= 2 and w_begun < 8 and (n - 2) % W_STEP == 0:
+            w_copies(w_begun // 2, w_begun % 2, "start")
+            w_begun += 1
         while prepared < GROUPS and ready[(META, prepared)] <= n:
             prepare(prepared)
             prepared += 1
@@ -637,7 +653,7 @@
 
 def on_device(grad_out, routes, probs, vision, pre_text, pre_vision, down_text, down_vision):
     gpt, gpv, gdt, gdv, gp = owner_kernel(
-        grad_out, routes.T, probs.T.astype(jnp.float32), vision[None, :],
+        grad_out, routes.T, probs.T, vision[None, :],
         down_text, down_vision, pre_text, pre_vision,
     )
     return gpt, gpv, gdt, gdv, gp.T

time: 144 us -> 142 us (0.986)
  no operation moved by 1% of the time
where the time goes in v3:
time: 142 us
  Pallas kernels  131 us (92%)
  local copies, waits for them, and re-layouts  10.2 us (7%)
    pallas_call x1, Pallas kernels, owner_kernel(): pl.pallas_call(body, out_shape=(like(pre_text.shape, bf16), like(pre_visi...  131 us
    unnamed x17, local copies, waits for them, and re-layouts  10.2 us

profile of v3, /device:TPU:6, one launch (start us, length us, event | category | flops | bytes accessed | tf_op | source)
XLA Modules:
  0.0 142.0 jit_solution(15638926493639883196)
XLA Ops:
  0.6 0.0 copy-start.1
  0.6 2.1 %copy.14.pv_ref = bf16[1,1,2,32,28,96]{5,4,3,2,1,0:T(8,128)(2,1)} copy(bf16[1,1,2,32,28,96]{5,3,4,2,1,0:T(8,128)(2,1)} %param.13) | data formatting | bytes 688128 | tf_op args[5]
  2.7 0.0 copy-done.1
  2.7 1.5 %copy.13.pt_ref = bf16[1,1,2,32,28,224]{5,4,3,2,1,0:T(8,128)(2,1)} copy(bf16[1,1,2,32,28,224]{5,3,4,2,1,0:T(8,128)(2,1)S(1)} %copy-done.1) | data formatting | bytes 1605632 | tf_op args[4]
  4.2 131.1 %shard_map.119 = (bf16[1,1,2,32,28,224]{5,4,3,2,1,0:T(8,128)(2,1)}, bf16[1,1,2,32,28,96]{5,4,3,2,1,0:T(8,128)(2,1)}, bf16[1,224,2048]{2,1,0:T(8,128)(2,1)}, bf16[1,96,2048]{2,1,0:T(8,128)(2,1)}, f32[8,128]{1,0:T(8,128)}) custom-call(bf16[128,512]{1,0:T(8,128)(2,1)} %g_ref.1, s32[8,128]{1,0:T(8,128)} %bitcast.5, bf16[8,128]{1,0:T(8,128)(2,1)} %bitcast.6, ...), custom_call_target="tpu_custom_call" | custom-call | flops 7000000000 | bytes 10000000 | tf_op jit(solution)/shard_map/pallas_call | solution.py:616
  135.3 0.0 copy-start.2
  135.3 2.7 %copy.15 = bf16[1,1,2,32,28,224]{5,3,4,2,1,0:T(8,128)(2,1)} copy(bf16[1,1,2,32,28,224]{5,4,3,2,1,0:T(8,128)(2,1)} %get-tuple-element.15) | data formatting | bytes 1605632
  138.1 0.0 copy-done.2
  138.1 0.0 copy-start
  138.1 0.9 copy.16
  139.0 0.4 copy-done
  139.4 0.0 copy-start.3
  139.4 0.9 copy.20
  140.3 0.3 copy-done.3
  140.6 0.0 copy-start.4
  140.6 0.7 copy.21
  141.4 0.0 copy-done.4
  141.4 0.6 copy.22
Async XLA Ops:
  0.6 2.1 %copy-start.1 = (bf16[1,1,2,32,28,224]{5,3,4,2,1,0:T(8,128)(2,1)S(1)}, bf16[1,1,2,32,28,224]{5,3,4,2,1,0:T(8,128)(2,1)}, u32[]{:S(2)}) copy-start(bf16[1,1,2,32,28,224]{5,3,4,2,1,0:T(8,128)(2,1)} %param.12) | copy-start | bytes 2408452
  135.3 2.7 %copy-start.2 = (bf16[1,1,2,32,28,96]{5,4,3,2,1,0:T(8,128)(2,1)S(1)}, bf16[1,1,2,32,28,96]{5,4,3,2,1,0:T(8,128)(2,1)}, u32[]{:S(2)}) copy-start(bf16[1,1,2,32,28,96]{5,4,3,2,1,0:T(8,128)(2,1)} %get-tuple-element.16) | copy-start | bytes 1032196
  138.1 1.3 copy-start
  139.4 1.2 copy-start.3
  140.6 0.8 copy-start.4
